TPU v7x, 32 devices: a whole 2x2x4 slice. The times are simulated.
32 devices in a mesh: row: 8 (over z, core), col: 4 (over y, x).
Axes of the slice: x: 2, y: 2, z: 4, core: 2. Of those that a mesh axis runs over, the one named last changes fastest.
Arguments:
- features: bfloat16 [4096, 128], P(('row', 'col')), may hold values from -6 to 6
- tiles: bfloat16 [8, 4, 32, 128, 128], P('row', 'col'), may hold values from -0.125 to 0.125
- tile_index: int32 [8, 4, 32], P('row', 'col'), may hold values from 0 to 31, as said below
- tile_count: int32 [8, 4], P('row', 'col'), may hold values from 4 to 32, as said below
- w_first: bfloat16 [128, 256], replicated, may hold values from -0.5 to 0.5
- b_first: float32 [256], replicated, may hold values from -3 to 3
- w_second: bfloat16 [256, 128], replicated, may hold values from -0.375 to 0.375
- b_second: float32 [128], replicated, may hold values from -3 to 3
Outputs:
- logits: float32 [4096, 128], P(('row', 'col'))
Inputs may be any that keep to these rules, and one draw needn't show every extreme that they name: `tile_index`: within one device the live slots name distinct tiles. `tile_count`: some device has all 32 slots live; every count is 32 divided by 1, 2, 4 or 8.
All inputs are finite; a program needn't handle non-finite values.
Results may differ from a plain program's by a relative error of at most 0.01.
Values may be sent and summed in bfloat16 or wider, within the bound.
A program may use at most 64 MiB of HBM per device.

v0:
```python
import jax
import jax.numpy as jnp
from jax import lax
from jax.sharding import PartitionSpec as P


def tile_sum(columns, tile_block, slot_index, live_count, node_rows):
    tile_size = tile_block.shape[-1]
    feat_width = columns.shape[1]
    col_tiles = columns.reshape(columns.shape[0] // tile_size, tile_size, feat_width)
    tile_cols = col_tiles.shape[0]
    row_tiles = lax.axis_size("col") * node_rows // tile_size
    picked = jnp.take(col_tiles, slot_index % tile_cols, axis=0)
    products = jnp.einsum("mab,mbf->maf", tile_block, picked, preferred_element_type=jnp.float32)
    live_mask = jnp.arange(slot_index.shape[0], dtype=jnp.int32) < live_count
    placing = (
        ((slot_index // tile_cols)[:, None] == jnp.arange(row_tiles, dtype=jnp.int32)[None, :])
        & live_mask[:, None]
    ).astype(jnp.float32)
    partial_value = jnp.einsum("mr,maf->raf", placing, products)
    return partial_value.reshape(row_tiles * tile_size, feat_width)


def aggregate(node_feats, tile_block, slot_index, live_count):
    node_rows = node_feats.shape[0]
    gathered = lax.all_gather(node_feats, "row", axis=0, tiled=True)
    partial_value = tile_sum(gathered, tile_block, slot_index, live_count, node_rows)
    return lax.psum_scatter(partial_value, "col", scatter_dimension=0, tiled=True)


def local(features, tiles, tile_index, tile_count, w_first, b_first, w_second, b_second):
    tile_block = tiles[0, 0]
    slot_index = tile_index[0, 0]
    live_count = tile_count[0, 0]
    first_agg = aggregate(features, tile_block, slot_index, live_count).astype(jnp.bfloat16)
    hidden = jnp.maximum(
        jnp.dot(first_agg, w_first, preferred_element_type=jnp.float32) + b_first, 0.0
    ).astype(jnp.bfloat16)
    projected = jnp.dot(hidden, w_second, preferred_element_type=jnp.float32).astype(jnp.bfloat16)
    second = aggregate(projected, tile_block, slot_index, live_count)
    return second + b_second


def solution(mesh):
    in_specs = (
        P(("row", "col"), None),
        P("row", "col", None, None, None),
        P("row", "col", None),
        P("row", "col"),
        P(),
        P(),
        P(),
        P(),
    )
    out_specs = P(("row", "col"), None)
    return jax.shard_map(local, mesh=mesh, in_specs=in_specs, out_specs=out_specs, check_vma=False)
```

profile of v0, /device:TPU:0, one launch (start us, length us, event | category | flops | bytes accessed | tf_op | source)
XLA Modules:
  0.0 104.9 jit_solution(11421321210908472564)
XLA Ops:
  6.5 0.0 copy-start
  6.5 0.0 copy-start.5
  6.5 0.0 reduce-scatter.3.cloned.1.call-start
  6.5 0.8 compare_and_fusion
  7.3 0.0 copy-done.5
  7.3 16.1 %all_gather.6 = bf16[1024,128]{1,0:T(8,128)(2,1)S(1)} all-gather(bf16[128,128]{1,0:T(8,128)(2,1)} %param.10), channel_id=1, replica_groups=mesh['row'=8,'col'=4] {'row'}, dimensions={0}, use_global_device_ids=true | all-gather | bytes 294912 | tf_op jit(solution)/shard_map/all_gather | solution.py:26
  23.4 0.7 gather_fusion
  24.2 0.0 copy-done
  24.2 1.0 fusion.10
  25.2 1.0 copy.11
  26.9 0.3 fusion.2
  27.1 0.7 copy.9
  27.8 0.0 copy-start.1
  27.8 0.0 copy-start.2
  27.8 0.0 copy-start.3
  27.8 0.0 reduce-scatter.3.cloned.1.call-update
  27.9 0.0 reduce-scatter.5.cloned.1.call-start
  27.9 25.3 %reduce-scatter.3.cloned.1.call-done = f32[128,128]{1,0:T(8,128)} async-done(((f32[512,128]{1,0:T(8,128)}), f32[128,128]{1,0:T(8,128)}) %reduce-scatter.3.cloned.1.call-update) | async-done | bytes 65552 | tf_op jit(solution)/shard_map/reduce_scatter | solution.py:28
  53.2 0.0 copy-done.1
  53.2 0.0 copy-done.2
  53.2 0.0 copy-done.3
  53.2 1.1 %fusion.7 = bf16[128,128]{1,0:T(8,128)(2,1)S(1)} fusion(bf16[256,128]{1,0:T(8,128)(2,1)S(1)} %copy-done.1, bf16[128,256]{1,0:T(8,128)(2,1)S(1)} %copy-done.2, f32[256]{0:T(256)S(1)} %copy-done.3, f32[128,128]{1,0:T(8,128)} %reduce-scatter.3.cloned.1.call-done), kind=kOutput, calls=%fused_computation.10 | convolution fusion | flops 16908288 | bytes 230400 | tf_op jit(solution)/shard_map/dot_general | solution.py:39
  54.3 14.3 %all_gather.7 = bf16[1024,128]{1,0:T(8,128)(2,1)S(1)} all-gather(bf16[128,128]{1,0:T(8,128)(2,1)S(1)} %fusion.7), channel_id=1, replica_groups=mesh['row'=8,'col'=4] {'row'}, dimensions={0}, use_global_device_ids=true | all-gather | bytes 294912 | tf_op jit(solution)/shard_map/all_gather | solution.py:26
  68.6 0.7 gather_fusion.1
  69.4 1.0 fusion.8
  70.4 1.0 copy.12
  71.4 0.3 fusion
  71.6 0.7 copy.10
  72.3 0.0 reduce-scatter.5.cloned.1.call-update
  72.4 24.2 %reduce-scatter.5.cloned.1.call-done = f32[128,128]{1,0:T(8,128)} async-done(((f32[512,128]{1,0:T(8,128)}), f32[128,128]{1,0:T(8,128)}) %reduce-scatter.5.cloned.1.call-update) | async-done | bytes 65552 | tf_op jit(solution)/shard_map/reduce_scatter | solution.py:28
  96.6 0.0 copy-done.4
  96.6 1.5 %broadcast_add_fusion = f32[128,128]{1,0:T(8,128)} fusion(f32[128,128]{1,0:T(8,128)} %reduce-scatter.5.cloned.1.call-done, f32[128]{0:T(128)S(1)} %copy-done.4), kind=kLoop, calls=%fused_computation.23 | loop fusion | flops 16384 | bytes 131584 | tf_op jit(solution)/shard_map/add | solution.py:41
  (4 shorter events, 0.0 us)
Async XLA Ops:
  6.5 17.7 %copy-start = (bf16[1,1,32,128,128]{4,3,2,1,0:T(8,128)(2,1)S(1)}, bf16[1,1,32,128,128]{4,3,2,1,0:T(8,128)(2,1)}, u32[]{:S(2)}) copy-start(bf16[1,1,32,128,128]{4,3,2,1,0:T(8,128)(2,1)} %param.11) | copy-start | bytes 3145732
  6.5 0.8 copy-start.5
  6.5 46.6 %reduce-scatter.3.cloned.1.call-start = ((), (), s32[]{:S(2)}) async-start(), calls=%async_computation.2 | async-start | bytes 327680 | tf_op jit(solution)/shard_map/reduce_scatter | solution.py:28
  27.8 25.3 %copy-start.1 = (bf16[256,128]{1,0:T(8,128)(2,1)S(1)}, bf16[256,128]{1,0:T(8,128)(2,1)}, u32[]{:S(2)}) copy-start(bf16[256,128]{1,0:T(8,128)(2,1)} %param.16) | copy-start | bytes 196612
  27.8 25.3 %copy-start.2 = (bf16[128,256]{1,0:T(8,128)(2,1)S(1)}, bf16[128,256]{1,0:T(8,128)(2,1)}, u32[]{:S(2)}) copy-start(bf16[128,256]{1,0:T(8,128)(2,1)} %param.14) | copy-start | bytes 196612
  27.8 25.3 %copy-start.3 = (f32[256]{0:T(256)S(1)}, f32[256]{0:T(256)}, u32[]{:S(2)}) copy-start(f32[256]{0:T(256)} %param.15) | copy-start | bytes 3076
  27.9 68.7 %reduce-scatter.5.cloned.1.call-start = ((), (), s32[]{:S(2)}) async-start(), calls=%async_computation.3 | async-start | bytes 327680 | tf_op jit(solution)/shard_map/reduce_scatter | solution.py:28
  72.3 24.2 %copy-start.4 = (f32[128]{0:T(128)S(1)}, f32[128]{0:T(128)}, u32[]{:S(2)}) copy-start(f32[128]{0:T(128)} %param.17) | copy-start | bytes 1540
Sparse Core Ops, SparseCore 0:
  28.0 25.1 reduce-scatter.2
  72.5 24.0 reduce-scatter.4
where the time goes:
time: 105 us
  waiting for transfers between devices  49.5 us (47%)
  blocking collectives  30.4 us (29%)
  between operations  14.1 us (13%)
  local copies, waits for them, and re-layouts  4.91 us (5%)
  matrix products  3.61 us (3%)
  other arithmetic  2.26 us (2%)
    reduce_scatter x2, waiting for transfers between devices, aggregate(): lax.psum_scatter(partial_value, 'col', scatter_dimension=0, tiled=True)  49.5 us
    all_gather x2, blocking collectives, aggregate(): gathered = lax.all_gather(node_feats, 'row', axis=0, tiled=True)  30.4 us
  transfers between devices with their start and end apart: 2, of which 2 were waited for; matrix products, arithmetic and copies ran while one was open for 0% of the time, Pallas kernels for 0%

commit v1 on v0

--- a/solution.py
+++ b/solution.py
@@ -1,7 +1,13 @@
+import functools
+
 import jax
 import jax.numpy as jnp
 from jax import lax
+from jax.experimental import pallas as pl
+from jax.experimental.pallas import tpu as pltpu
 from jax.sharding import PartitionSpec as P
+
+CORES = 2
 
 
 def tile_sum(columns, tile_block, slot_index, live_count, node_rows):
@@ -28,7 +34,7 @@
     return lax.psum_scatter(partial_value, "col", scatter_dimension=0, tiled=True)
 
 
-def local(features, tiles, tile_index, tile_count, w_first, b_first, w_second, b_second):
+def sparse_local(features, tiles, tile_index, tile_count, w_first, b_first, w_second, b_second):
     tile_block = tiles[0, 0]
     slot_index = tile_index[0, 0]
     live_count = tile_count[0, 0]
@@ -41,6 +47,182 @@
     return second + b_second
 
 
+def kernel(
+    n_row, n_col,
+    feats, tiles, index, count, w1, b1, w2, b2, out,
+    tiles_v, index_s, count_s, w1_v, b1_v, w2_v, b2_v, adj, x1, x2,
+    part_out, part_in,
+    local_sem, gather_send, gather_recv, sib_send, sib_recv, part_send, part_recv,
+):
+    node_rows = feats.shape[0]
+    slots, tile = tiles.shape[2], tiles.shape[3]
+    n_chip = n_row // CORES
+    tile_cols = n_row * node_rows // tile
+    row, col = lax.axis_index("row"), lax.axis_index("col")
+    chip, core = lax.div(row, CORES), lax.rem(row, CORES)
+    sibling = chip * CORES + (1 - core)
+
+    def at_chip(step):
+        return lax.rem(chip + step + n_chip, n_chip) * CORES + core
+
+    def at_col(step):
+        return lax.rem(col + step + n_col, n_col)
+
+    def rows(block):
+        return pl.ds(pl.multiple_of(block * node_rows, node_rows), node_rows)
+
+    loads = [
+        pltpu.make_async_copy(index, index_s, local_sem.at[0]),
+        pltpu.make_async_copy(count, count_s, local_sem.at[1]),
+        pltpu.make_async_copy(tiles.at[0, 0], tiles_v.at[pl.ds(0, slots)], local_sem.at[2]),
+        pltpu.make_async_copy(feats, x1.at[rows(row)], local_sem.at[3]),
+        pltpu.make_async_copy(w1, w1_v, local_sem.at[4]),
+        pltpu.make_async_copy(b1, b1_v, local_sem.at[5]),
+        pltpu.make_async_copy(w2, w2_v, local_sem.at[6]),
+        pltpu.make_async_copy(b2, b2_v, local_sem.at[7]),
+    ]
+
+    barrier = pltpu.get_barrier_semaphore()
+    greeted = [{"row": at_chip(k), "col": col} for k in range(1, n_chip)]
+    greeted += [{"row": sibling, "col": col}]
+    greeted += [{"row": row, "col": at_col(k)} for k in range(1, n_col)]
+    for device in greeted:
+        pl.semaphore_signal(barrier, inc=1, device_id=device, device_id_type=pl.DeviceIdType.MESH)
+    for load in loads:
+        load.start()
+    pl.semaphore_wait(barrier, len(greeted))
+
+    def remote(src, dst, send_sem, recv_sem, device):
+        return pltpu.make_async_remote_copy(
+            src_ref=src, dst_ref=dst, send_sem=send_sem, recv_sem=recv_sem,
+            device_id=device, device_id_type=pl.DeviceIdType.MESH,
+        )
+
+    def gather_start(layer, src, x):
+        sends = []
+        for k in range(1, n_chip):
+            sends.append(remote(
+                src, x.at[rows(row)], gather_send.at[layer, k - 1], gather_recv.at[layer, k - 1],
+                {"row": at_chip(k), "col": col},
+            ))
+        sends.append(remote(
+            src, x.at[rows(row)], sib_send.at[layer, 0], sib_recv.at[layer, 0],
+            {"row": sibling, "col": col},
+        ))
+        for send in sends:
+            send.start()
+        return sends
+
+    def gather_finish(layer, x, sends):
+        for k in range(1, n_chip):
+            sends[k - 1].wait_recv()
+            block = x.at[rows(at_chip(-k))]
+            forward = remote(
+                block, block, sib_send.at[layer, k], sib_recv.at[layer, k],
+                {"row": sibling, "col": col},
+            )
+            forward.start()
+            sends.append(forward)
+        for send in sends[n_chip - 1:]:
+            send.wait_recv()
+
+    def reduce_scatter(layer, x):
+        sends = []
+        for k in range(1, n_col):
+            target = at_col(k)
+            part_out[layer, k - 1] = jnp.dot(
+                adj[rows(target), :], x[...], preferred_element_type=jnp.float32
+            ).astype(part_out.dtype)
+            send = remote(
+                part_out.at[layer, k - 1], part_in.at[layer, k - 1],
+                part_send.at[layer, k - 1], part_recv.at[layer, k - 1],
+                {"row": row, "col": target},
+            )
+            send.start()
+            sends.append(send)
+        total = jnp.dot(adj[rows(col), :], x[...], preferred_element_type=jnp.float32)
+        for k in range(1, n_col):
+            sends[k - 1].wait_recv()
+            total = total + part_in[layer, k - 1].astype(jnp.float32)
+        return total, sends
+
+    first_sends = gather_start(0, feats, x1)
+
+    tiles_v[slots] = jnp.zeros(tiles_v.shape[1:], tiles_v.dtype)
+    for load in loads[:4]:
+        load.wait()
+    live = count_s[0, 0]
+
+    def place(position, carry):
+        found = jnp.int32(slots)
+        for slot in range(slots):
+            hit = (index_s[0, 0, slot] == position) & (slot < live)
+            found = jnp.where(hit, jnp.int32(slot), found)
+        r = lax.div(position, tile_cols)
+        c = lax.rem(position, tile_cols)
+        adj[
+            pl.ds(pl.multiple_of(r * tile, tile), tile), pl.ds(pl.multiple_of(c * tile, tile), tile)
+        ] = tiles_v[found]
+        return carry
+
+    lax.fori_loop(0, adj.shape[0] // tile * tile_cols, place, 0)
+
+    gather_finish(0, x1, first_sends)
+    total, first_parts = reduce_scatter(0, x1)
+    for load in loads[4:]:
+        load.wait()
+    hidden = jnp.maximum(
+        jnp.dot(total.astype(jnp.bfloat16), w1_v[...], preferred_element_type=jnp.float32)
+        + b1_v[...].reshape(1, -1), 0.0
+    ).astype(jnp.bfloat16)
+    x2[rows(row), :] = jnp.dot(hidden, w2_v[...], preferred_element_type=jnp.float32).astype(jnp.bfloat16)
+
+    second_sends = gather_start(1, x2.at[rows(row)], x2)
+    gather_finish(1, x2, second_sends)
+    total, second_parts = reduce_scatter(1, x2)
+    out[...] = total + b2_v[...].reshape(1, -1)
+    for send in first_sends + first_parts + second_sends + second_parts:
+        send.wait_send()
+
+
+def dense_local(n_row, n_col, features, tiles, tile_index, tile_count, w_first, b_first, w_second, b_second):
+    node_rows, f_in = features.shape
+    slots, tile = tiles.shape[2], tiles.shape[3]
+    width = w_second.shape[1]
+    n_chip = n_row // CORES
+    dma = pltpu.SemaphoreType.DMA
+    return pl.pallas_call(
+        functools.partial(kernel, n_row, n_col),
+        out_shape=jax.ShapeDtypeStruct((node_rows, width), jnp.float32),
+        in_specs=[pl.BlockSpec(memory_space=pl.ANY)] * 8,
+        out_specs=pl.BlockSpec(memory_space=pltpu.VMEM),
+        scratch_shapes=[
+            pltpu.VMEM((slots + 1, tile, tile), tiles.dtype),
+            pltpu.SMEM(tile_index.shape, jnp.int32),
+            pltpu.SMEM(tile_count.shape, jnp.int32),
+            pltpu.VMEM(w_first.shape, w_first.dtype),
+            pltpu.VMEM(b_first.shape, b_first.dtype),
+            pltpu.VMEM(w_second.shape, w_second.dtype),
+            pltpu.VMEM(b_second.shape, b_second.dtype),
+            pltpu.VMEM((n_col * node_rows, n_row * node_rows), tiles.dtype),
+            pltpu.VMEM((n_row * node_rows, f_in), jnp.bfloat16),
+            pltpu.VMEM((n_row * node_rows, width), jnp.bfloat16),
+            pltpu.VMEM((2, n_col - 1, node_rows, width), jnp.bfloat16),
+            pltpu.VMEM((2, n_col - 1, node_rows, width), jnp.bfloat16),
+            dma((8,)),
+            dma((2, n_chip - 1)),
+            dma((2, n_chip - 1)),
+            dma((2, n_chip)),
+            dma((2, n_chip)),
+            dma((2, n_col - 1)),
+            dma((2, n_col - 1)),
+        ],
+        compiler_params=pltpu.CompilerParams(
+            collective_id=0, has_side_effects=True, vmem_limit_bytes=16 * 2**20
+        ),
+    )(features, tiles, tile_index, tile_count, w_first, b_first, w_second, b_second)
+
+
 def solution(mesh):
     in_specs = (
         P(("row", "col"), None),
@@ -53,4 +235,17 @@
         P(),
     )
     out_specs = P(("row", "col"), None)
+    n_row, n_col = mesh.shape["row"], mesh.shape["col"]
+
+    def local(features, tiles, *rest):
+        node_rows, (slots, tile) = features.shape[0], tiles.shape[2:4]
+        positions = (n_row * node_rows // tile) * (n_col * node_rows // tile)
+        fits = (
+            n_row % CORES == 0 and n_row > CORES and n_col > 1 and node_rows % tile == 0
+            and features.shape[1] == rest[4].shape[1] and positions <= 2 * slots
+        )
+        if fits:
+            return dense_local(n_row, n_col, features, tiles, *rest)
+        return sparse_local(features, tiles, *rest)
+
     return jax.shard_map(local, mesh=mesh, in_specs=in_specs, out_specs=out_specs, check_vma=False)

time: 105 us -> 29.8 us (0.28)
  waiting for transfers between devices: 49.5 us -> 0 us
  blocking collectives: 30.4 us -> 0 us
  Pallas kernels: 0 us -> 23.8 us
  between operations: 14.1 us -> 0.72 us
  matrix products: 3.61 us -> 0 us
  other arithmetic: 2.26 us -> 0 us
    reduce_scatter x2 -> x0, waiting for transfers between devices: 49.5 us -> none  [aggregate(): lax.psum_scatter(partial_value, 'col', scatter_dimension=0, tiled=True)]
    all_gather x2 -> x0, blocking collectives: 30.4 us -> none  [aggregate(): gathered = lax.all_gather(node_feats, 'row', axis=0, tiled=True)]
    pallas_call x0 -> x1, Pallas kernels: none -> 23.8 us  [dense_local(): pl.pallas_call(functools.partial(kernel, n_row, n_col), out_shape=jax.Sha...]
    unnamed x12 -> x15, local copies, waits for them, and re-layouts: 0.02 us -> 4.95 us
    dot_general x5 -> x0, matrix products: 3.61 us -> none  [the longest x2 1.99 us: tile_sum(): jnp.einsum('mab,mbf->maf', tile_block, picked, preferred_element_type=jnp...]
    dot_general x4 -> x0, local copies, waits for them, and re-layouts: 3.39 us -> none  [the longest x2 1.95 us: tile_sum(): jnp.einsum('mab,mbf->maf', tile_block, picked, preferred_element_type=jnp...]
    gather x2 -> x0, local copies, waits for them, and re-layouts: 1.49 us -> none  [tile_sum(): picked = jnp.take(col_tiles, slot_index % tile_cols, axis=0)]
    add x1 -> x0, other arithmetic: 1.47 us -> none  [local(): return second + b_second]
  transfers between devices with their start and end apart: 2 -> 0, of which waited for: 2 -> 0; matrix products, arithmetic and copies ran while one was open for 0% -> 0% of each run, Pallas kernels for 0% -> 0%
where the time goes in v1:
time: 29.8 us; the launch traced here: 29.5 us
  Pallas kernels  23.8 us (80%)
  local copies, waits for them, and re-layouts  4.95 us (17%)
  between operations  0.72 us (2%)
    pallas_call x1, Pallas kernels, dense_local(): pl.pallas_call(functools.partial(kernel, n_row, n_col), out_shape=jax.Sha...  23.8 us
    unnamed x15, local copies, waits for them, and re-layouts  4.95 us

profile of v1, /device:TPU:0, one launch (start us, length us, event | category | flops | bytes accessed | tf_op | source)
XLA Modules:
  0.0 29.5 jit_solution(2770720213841824793)
XLA Ops:
  0.0 0.0 copy-start.4
  0.0 0.0 copy-start.5
  0.7 0.0 copy-done.4
  0.7 0.0 copy-done.5
  0.7 0.0 copy-start
  0.7 1.2 %copy-done = bf16[1,1,32,128,128]{4,3,2,1,0:T(8,128)(2,1)S(1)} copy-done((bf16[1,1,32,128,128]{4,3,2,1,0:T(8,128)(2,1)S(1)}, bf16[1,1,32,128,128]{4,3,2,1,0:T(8,128)(2,1)}, u32[]{:S(2)}) %copy-start) | copy-done | bytes 1048600
  1.9 0.0 copy-start.1
  1.9 0.8 %copy-done.1 = bf16[128,256]{1,0:T(8,128)(2,1)S(1)} copy-done((bf16[128,256]{1,0:T(8,128)(2,1)S(1)}, bf16[128,256]{1,0:T(8,128)(2,1)}, u32[]{:S(2)}) %copy-start.1) | copy-done | bytes 65560
  2.8 0.0 copy-start.2
  2.8 0.8 %copy-done.2 = bf16[256,128]{1,0:T(8,128)(2,1)S(1)} copy-done((bf16[256,128]{1,0:T(8,128)(2,1)S(1)}, bf16[256,128]{1,0:T(8,128)(2,1)}, u32[]{:S(2)}) %copy-start.2) | copy-done | bytes 65560
  3.6 0.0 copy-start.3
  3.6 0.8 %copy-done.3 = bf16[128,128]{1,0:T(8,128)(2,1)S(1)} copy-done((bf16[128,128]{1,0:T(8,128)(2,1)S(1)}, bf16[128,128]{1,0:T(8,128)(2,1)}, u32[]{:S(2)}) %copy-start.3) | copy-done | bytes 32792
  4.4 0.0 copy-start.6
  4.4 0.7 %copy-done.6 = f32[128]{0:T(128)S(1)} copy-done((f32[128]{0:T(128)S(1)}, f32[128]{0:T(128)}, u32[]{:S(2)}) %copy-start.6) | copy-done | bytes 536
  5.0 23.8 %shard_map.82 = f32[128,128]{1,0:T(8,128)S(1)} custom-call(bf16[128,128]{1,0:T(8,128)(2,1)S(1)} %copy-done.3, bf16[1,1,32,128,128]{4,3,2,1,0:T(8,128)(2,1)S(1)} %copy-done, s32[1,1,32]{2,1,0:T(1,128)S(1)} %copy-done.5, s32[1,1]{1,0:T(1,128)S(6)} %copy.10.count, bf16[128,256]{1,0:T(8,128)(2,1)S(1)} %copy-done.1, f32[256]{0:T(256)S(1)} %copy-done.4, ...), custom_call_target="tpu_custom_call" | custom-call | tf_op jit(solution)/shard_map/pallas_call | solution.py:194
  28.8 0.6 %copy.11 = f32[128,128]{1,0:T(8,128)} copy(f32[128,128]{1,0:T(8,128)S(1)} %shard_map.82) | data formatting | bytes 131072
Async XLA Ops:
  0.0 0.7 %copy-start.4 = (f32[256]{0:T(256)S(1)}, f32[256]{0:T(256)}, u32[]{:S(2)}) copy-start(f32[256]{0:T(256)} %b1.1) | copy-start | bytes 3076
  0.0 0.7 %copy-start.5 = (s32[1,1,32]{2,1,0:T(1,128)S(1)}, s32[1,1,32]{2,1,0:T(1,128)}, u32[]{:S(2)}) copy-start(s32[1,1,32]{2,1,0:T(1,128)} %index.1) | copy-start | bytes 388
  0.7 1.2 %copy-start = (bf16[1,1,32,128,128]{4,3,2,1,0:T(8,128)(2,1)S(1)}, bf16[1,1,32,128,128]{4,3,2,1,0:T(8,128)(2,1)}, u32[]{:S(2)}) copy-start(bf16[1,1,32,128,128]{4,3,2,1,0:T(8,128)(2,1)} %tiles.1) | copy-start | bytes 3145732
  1.9 0.8 %copy-start.1 = (bf16[128,256]{1,0:T(8,128)(2,1)S(1)}, bf16[128,256]{1,0:T(8,128)(2,1)}, u32[]{:S(2)}) copy-start(bf16[128,256]{1,0:T(8,128)(2,1)} %w1.1) | copy-start | bytes 196612
  2.8 0.8 %copy-start.2 = (bf16[256,128]{1,0:T(8,128)(2,1)S(1)}, bf16[256,128]{1,0:T(8,128)(2,1)}, u32[]{:S(2)}) copy-start(bf16[256,128]{1,0:T(8,128)(2,1)} %w2.1) | copy-start | bytes 196612
  3.6 0.8 %copy-start.3 = (bf16[128,128]{1,0:T(8,128)(2,1)S(1)}, bf16[128,128]{1,0:T(8,128)(2,1)}, u32[]{:S(2)}) copy-start(bf16[128,128]{1,0:T(8,128)(2,1)} %feats.1) | copy-start | bytes 98308
  4.4 0.7 %copy-start.6 = (f32[128]{0:T(128)S(1)}, f32[128]{0:T(128)}, u32[]{:S(2)}) copy-start(f32[128]{0:T(128)} %b2.1) | copy-start | bytes 1540

commit v2 on v1

--- a/solution.py
+++ b/solution.py
@@ -50,7 +50,7 @@
 def kernel(
     n_row, n_col,
     feats, tiles, index, count, w1, b1, w2, b2, out,
-    tiles_v, index_s, count_s, w1_v, b1_v, w2_v, b2_v, adj, x1, x2,
+    tiles_v, index_v, count_s, w1_v, b1_v, w2_v, b2_v, adj, x1, x2,
     part_out, part_in,
     local_sem, gather_send, gather_recv, sib_send, sib_recv, part_send, part_recv,
 ):
@@ -72,7 +72,7 @@
         return pl.ds(pl.multiple_of(block * node_rows, node_rows), node_rows)
 
     loads = [
-        pltpu.make_async_copy(index, index_s, local_sem.at[0]),
+        pltpu.make_async_copy(index, index_v, local_sem.at[0]),
         pltpu.make_async_copy(count, count_s, local_sem.at[1]),
         pltpu.make_async_copy(tiles.at[0, 0], tiles_v.at[pl.ds(0, slots)], local_sem.at[2]),
         pltpu.make_async_copy(feats, x1.at[rows(row)], local_sem.at[3]),
@@ -90,6 +90,16 @@
         pl.semaphore_signal(barrier, inc=1, device_id=device, device_id_type=pl.DeviceIdType.MESH)
     for load in loads:
         load.start()
+
+    tiles_v[slots] = jnp.zeros(tiles_v.shape[1:], tiles_v.dtype)
+    for load in loads[:2]:
+        load.wait()
+    n_pos = adj.shape[0] // tile * tile_cols
+    slot = lax.broadcasted_iota(jnp.int32, (n_pos, slots), 1)
+    position = lax.broadcasted_iota(jnp.int32, (n_pos, slots), 0)
+    hit = (index_v[0] == position) & (slot < count_s[0, 0])
+    slot_at = jnp.min(jnp.where(hit, slot, slots), axis=1, keepdims=True)
+
     pl.semaphore_wait(barrier, len(greeted))
 
     def remote(src, dst, send_sem, recv_sem, device):
@@ -148,24 +158,11 @@
 
     first_sends = gather_start(0, feats, x1)
 
-    tiles_v[slots] = jnp.zeros(tiles_v.shape[1:], tiles_v.dtype)
-    for load in loads[:4]:
+    for load in loads[2:4]:
         load.wait()
-    live = count_s[0, 0]
-
-    def place(position, carry):
-        found = jnp.int32(slots)
-        for slot in range(slots):
-            hit = (index_s[0, 0, slot] == position) & (slot < live)
-            found = jnp.where(hit, jnp.int32(slot), found)
-        r = lax.div(position, tile_cols)
-        c = lax.rem(position, tile_cols)
-        adj[
-            pl.ds(pl.multiple_of(r * tile, tile), tile), pl.ds(pl.multiple_of(c * tile, tile), tile)
-        ] = tiles_v[found]
-        return carry
-
-    lax.fori_loop(0, adj.shape[0] // tile * tile_cols, place, 0)
+    for place in range(n_pos):
+        r, c = place // tile_cols, place % tile_cols
+        adj[r * tile:(r + 1) * tile, c * tile:(c + 1) * tile] = tiles_v[slot_at[place, 0]]
 
     gather_finish(0, x1, first_sends)
     total, first_parts = reduce_scatter(0, x1)
@@ -194,11 +191,11 @@
     return pl.pallas_call(
         functools.partial(kernel, n_row, n_col),
         out_shape=jax.ShapeDtypeStruct((node_rows, width), jnp.float32),
-        in_specs=[pl.BlockSpec(memory_space=pl.ANY)] * 8,
+        in_specs=[pl.BlockSpec(memory_space=pltpu.HBM)] * 8,
         out_specs=pl.BlockSpec(memory_space=pltpu.VMEM),
         scratch_shapes=[
             pltpu.VMEM((slots + 1, tile, tile), tiles.dtype),
-            pltpu.SMEM(tile_index.shape, jnp.int32),
+            pltpu.VMEM(tile_index.shape, jnp.int32),
             pltpu.SMEM(tile_count.shape, jnp.int32),
             pltpu.VMEM(w_first.shape, w_first.dtype),
             pltpu.VMEM(b_first.shape, b_first.dtype),
@@ -218,7 +215,7 @@
             dma((2, n_col - 1)),
         ],
         compiler_params=pltpu.CompilerParams(
-            collective_id=0, has_side_effects=True, vmem_limit_bytes=16 * 2**20
+            collective_id=0, has_side_effects=True, vmem_limit_bytes=56 * 2**20
         ),
     )(features, tiles, tile_index, tile_count, w_first, b_first, w_second, b_second)
 

time: 29.8 us -> 27 us (0.906)
  local copies, waits for them, and re-layouts: 4.95 us -> 1.47 us
  Pallas kernels: 23.8 us -> 24.7 us
    unnamed x15 -> x1, local copies, waits for them, and re-layouts: 4.95 us -> 1.47 us
    pallas_call x1, Pallas kernels: 23.8 us -> 24.7 us  [dense_local(): pl.pallas_call(functools.partial(kernel, n_row, n_col), out_shape=jax.Sha...]
where the time goes in v2:
time: 27 us; the launch traced here: 26.8 us
  Pallas kernels  24.7 us (91%)
  local copies, waits for them, and re-layouts  1.47 us (5%)
  between operations  0.66 us (2%)
    pallas_call x1, Pallas kernels, dense_local(): pl.pallas_call(functools.partial(kernel, n_row, n_col), out_shape=jax.Sha...  24.7 us
    unnamed x1, local copies, waits for them, and re-layouts  1.47 us

profile of v2, /device:TPU:0, one launch (start us, length us, event | category | flops | bytes accessed | tf_op | source)
XLA Modules:
  0.0 26.8 jit_solution(8168950921940496874)
XLA Ops:
  0.7 24.7 %shard_map.82 = f32[128,128]{1,0:T(8,128)} custom-call(bf16[128,128]{1,0:T(8,128)(2,1)} %feats.1, bf16[1,1,32,128,128]{4,3,2,1,0:T(8,128)(2,1)} %tiles.1, s32[1,1,32]{2,1,0:T(1,128)} %index.1, s32[1,1]{1,0:T(1,128)S(6)} %copy.10.count, bf16[128,256]{1,0:T(8,128)(2,1)} %w1.1, f32[256]{0:T(256)} %b1.1, bf16[256,128]{1,0:T(8,128)(2,1)} %w2.1, f32[128]{0:T(128)} %b2.1), custom_call_target="tpu_custom_call" | custom-call | tf_op jit(solution)/shard_map/pallas_call | solution.py:191
  25.4 1.5 %copy.11 = f32[128,128]{1,0:T(8,128)} copy(f32[128,128]{1,0:T(8,128)} %shard_map.82) | data formatting | bytes 131072

commit v3 on v2

--- a/solution.py
+++ b/solution.py
@@ -119,8 +119,9 @@
             src, x.at[rows(row)], sib_send.at[layer, 0], sib_recv.at[layer, 0],
             {"row": sibling, "col": col},
         ))
-        for send in sends:
-            send.start()
+        sends[-1].start()
+        for k in range(1, n_chip):
+            sends[k - 1].start()
         return sends
 
     def gather_finish(layer, x, sends):
@@ -156,10 +157,10 @@
             total = total + part_in[layer, k - 1].astype(jnp.float32)
         return total, sends
 
-    first_sends = gather_start(0, feats, x1)
-
-    for load in loads[2:4]:
-        load.wait()
+    loads[3].wait()
+    first_sends = gather_start(0, x1.at[rows(row)], x1)
+
+    loads[2].wait()
     for place in range(n_pos):
         r, c = place // tile_cols, place % tile_cols
         adj[r * tile:(r + 1) * tile, c * tile:(c + 1) * tile] = tiles_v[slot_at[place, 0]]

time: 27 us -> 26.8 us (level)
  no operation moved by 1% of the time
where the time goes in v3:
time: 26.8 us; the launch traced here: 26.6 us
  Pallas kernels  24.5 us (91%)
  local copies, waits for them, and re-layouts  1.47 us (5%)
  between operations  0.66 us (2%)
    pallas_call x1, Pallas kernels, dense_local(): pl.pallas_call(functools.partial(kernel, n_row, n_col), out_shape=jax.Sha...  24.5 us
    unnamed x1, local copies, waits for them, and re-layouts  1.47 us

profile of v3, /device:TPU:0, one launch (start us, length us, event | category | flops | bytes accessed | tf_op | source)
XLA Modules:
  0.0 26.6 jit_solution(7240939194379755441)
XLA Ops:
  0.7 24.5 %shard_map.82 = f32[128,128]{1,0:T(8,128)} custom-call(bf16[128,128]{1,0:T(8,128)(2,1)} %feats.1, bf16[1,1,32,128,128]{4,3,2,1,0:T(8,128)(2,1)} %tiles.1, s32[1,1,32]{2,1,0:T(1,128)} %index.1, s32[1,1]{1,0:T(1,128)S(6)} %copy.10.count, bf16[128,256]{1,0:T(8,128)(2,1)} %w1.1, f32[256]{0:T(256)} %b1.1, bf16[256,128]{1,0:T(8,128)(2,1)} %w2.1, f32[128]{0:T(128)} %b2.1), custom_call_target="tpu_custom_call" | custom-call | tf_op jit(solution)/shard_map/pallas_call | solution.py:192
  25.1 1.5 %copy.11 = f32[128,128]{1,0:T(8,128)} copy(f32[128,128]{1,0:T(8,128)} %shard_map.82) | data formatting | bytes 131072

commit v4 on v3

--- a/solution.py
+++ b/solution.py
@@ -138,8 +138,8 @@
             send.wait_recv()
 
     def reduce_scatter(layer, x):
-        sends = []
-        for k in range(1, n_col):
+        sends = {}
+        for k in sorted(range(1, n_col), key=lambda k: -abs(2 * k - n_col)):
             target = at_col(k)
             part_out[layer, k - 1] = jnp.dot(
                 adj[rows(target), :], x[...], preferred_element_type=jnp.float32
@@ -150,12 +150,12 @@
                 {"row": row, "col": target},
             )
             send.start()
-            sends.append(send)
+            sends[k] = send
         total = jnp.dot(adj[rows(col), :], x[...], preferred_element_type=jnp.float32)
-        for k in range(1, n_col):
-            sends[k - 1].wait_recv()
+        for k in sends:
+            sends[k].wait_recv()
             total = total + part_in[layer, k - 1].astype(jnp.float32)
-        return total, sends
+        return total, list(sends.values())
 
     loads[3].wait()
     first_sends = gather_start(0, x1.at[rows(row)], x1)

time: 26.8 us -> 26.6 us (level)
  no operation moved by 1% of the time
where the time goes in v4:
time: 26.6 us; the launch traced here: 26.4 us
  Pallas kernels  24.3 us (91%)
  local copies, waits for them, and re-layouts  1.47 us (6%)
  between operations  0.66 us (2%)
    pallas_call x1, Pallas kernels, dense_local(): pl.pallas_call(functools.partial(kernel, n_row, n_col), out_shape=jax.Sha...  24.3 us
    unnamed x1, local copies, waits for them, and re-layouts  1.47 us

profile of v4, /device:TPU:0, one launch (start us, length us, event | category | flops | bytes accessed | tf_op | source)
XLA Modules:
  0.0 26.4 jit_solution(10864825671854993321)
XLA Ops:
  0.7 24.3 %shard_map.82 = f32[128,128]{1,0:T(8,128)} custom-call(bf16[128,128]{1,0:T(8,128)(2,1)} %feats.1, bf16[1,1,32,128,128]{4,3,2,1,0:T(8,128)(2,1)} %tiles.1, s32[1,1,32]{2,1,0:T(1,128)} %index.1, s32[1,1]{1,0:T(1,128)S(6)} %copy.10.count, bf16[128,256]{1,0:T(8,128)(2,1)} %w1.1, f32[256]{0:T(256)} %b1.1, bf16[256,128]{1,0:T(8,128)(2,1)} %w2.1, f32[128]{0:T(128)} %b2.1), custom_call_target="tpu_custom_call" | custom-call | tf_op jit(solution)/shard_map/pallas_call | solution.py:192
  24.9 1.5 %copy.11 = f32[128,128]{1,0:T(8,128)} copy(f32[128,128]{1,0:T(8,128)} %shard_map.82) | data formatting | bytes 131072
